TPU v7x, 256 devices: a whole 4x4x8 slice. The times are simulated.
256 devices in a mesh: gx: 32 (over y, x, core), gy: 8 (over z).
Axes of the slice: x: 4, y: 4, z: 8, core: 2. Of those that a mesh axis runs over, the one named last changes fastest.
Arguments:
- probes: float32 [64, 64, 64, 128], P(None, 'gx', 'gy'), may hold values from -6 to 6
- conduct: float32 [64, 64, 128], P('gx', 'gy'), may hold values from 0.25 to 2
- storage: float32 [64, 64, 128], P('gx', 'gy'), may hold values from 0.5 to 2
Outputs:
- basis: float32 [64, 64, 64, 128], P(None, 'gx', 'gy')
- factor: float32 [64, 64], replicated
All inputs are finite; a program needn't handle non-finite values.
Results may differ from a plain program's by a relative error of at most 0.00005.
Values sent between devices are 32-bit elements; how exact they have to be, the bound alone decides.
No kernel may reach another device: no remote copies, remote signals or barrier semaphores. Data moves between devices by JAX's collectives and lax.ppermute only.
A program may use at most 64 MiB of HBM per device.

v0:
```python
import functools
import math

import jax
import jax.numpy as jnp
from jax import lax
from jax.experimental import pallas as pl
from jax.experimental.pallas import tpu as pltpu
from jax.sharding import Mesh, PartitionSpec as P

STEPS = 8
time_step = 0.07
prior_weight = 0.5

OWN = 8
EXT = 3 * OWN
CHUNK = 40

f32 = jnp.float32


def send_kernel(probes_hbm, conduct_hbm, storage_hbm, out, probes, conduct, storage, sems):
    pairs = ((storage_hbm, storage), (probes_hbm, probes), (conduct_hbm, conduct))
    copies = [pltpu.make_async_copy(a, b, sems.at[i]) for i, (a, b) in enumerate(pairs)]
    for copy in copies:
        copy.start()
    for copy in copies:
        copy.wait()
    weight = time_step * storage[...]
    for g in range(32):
        out[g, 0:16] = weight * probes[2 * g]
        out[g, 16:32] = weight * probes[2 * g + 1]
        out[g, 32:40] = conduct[8 * (g % 2):8 * (g % 2) + 8]


def pack_kernel(got, half, first):
    for y in range(OWN):
        for i in range(4):
            half[y, i] = got[pl.ds(i * CHUNK + 32 + y, 8, stride=4 * CHUNK)]
        for j in range(8):
            first[y, j] = got[pl.ds((j // 2) * CHUNK + (j % 2) * 8 + y, 8, stride=4 * CHUNK)]


def pack_second_kernel(got, arrived, out):
    for y in range(OWN):
        for j in range(8):
            out[y, j] = got[pl.ds((j // 2) * CHUNK + 16 + (j % 2) * 8 + y, 8, stride=4 * CHUNK)]


def strips(own, pair, other):
    odd = lax.rem(lax.axis_index("tz"), 2)
    return ((own, OWN), (pair, 2 * OWN * (1 - odd)), (other, 2 * OWN * odd))


def coef_kernel(m0, m1, m2, t0, t1, t2, coef, stay):
    core = lax.axis_index("tc")
    for (mine, theirs), row in strips((m0, t0), (m1, t1), (m2, t2)):
        for y in range(OWN):
            for i in range(4):
                for v, j in ((mine[y, i], 2 * i + core), (theirs[y, i], 2 * i + 1 - core)):
                    a = time_step * v
                    coef[row + y, j] = a
                    stay[row + y, j] = 1.0 - 6.0 * a


def masks():
    sub = lax.broadcasted_iota(jnp.int32, (8, 128), 0)
    return band(), None, sub == 0, sub == 7


def put(buf, y, vals, m):
    for j in range(8):
        buf[y, j + 1] = vals[j]
    buf[y, 0] = jnp.where(m[2], 0.0, pltpu.roll(vals[7], 1, 0))
    buf[y, 9] = jnp.where(m[3], 0.0, pltpu.roll(vals[0], 7, 0))


def band():
    row = lax.broadcasted_iota(jnp.int32, (256, 128), 0) % 128
    col = lax.broadcasted_iota(jnp.int32, (256, 128), 1)
    return jnp.where(jnp.abs(row - col) == 1, 1.0, 0.0).astype(jnp.bfloat16)


def row_sums(buf, y, m):
    row = [buf[y, j] for j in range(10)]
    whole = jnp.concatenate(row[1:9], axis=0)
    high = whole.astype(jnp.bfloat16)
    low = (whole - high.astype(f32)).astype(jnp.bfloat16)
    along = jnp.dot(jnp.concatenate([high, low], axis=1), m[0], preferred_element_type=f32)
    out = []
    for j in range(8):
        s = (buf[y - 1, j + 1] + buf[y + 1, j + 1]) + (row[j] + row[j + 2]) + along[8 * j:8 * j + 8]
        out.append((row[j + 1], s))
    return out


def forward_kernel(own, pair, other, coef, stay, out, scaled, ping, pong):
    m = masks()
    for ref, row in strips(own, pair, other):
        for y in range(OWN):
            vals = []
            for j in range(8):
                v = coef[row + y, j] * ref[y, j]
                scaled[row + y, j] = v
                vals.append(v)
            put(ping, row + y, vals, m)
    bufs = (ping, pong)
    for k in range(1, STEPS):
        now, later = bufs[(k - 1) % 2], bufs[k % 2]
        for y in range(k, EXT - k):
            vals = []
            for j, (c, s) in enumerate(row_sums(now, y, m)):
                vals.append((scaled[y, j] + stay[y, j] * c) + coef[y, j] * s)
            put(later, y, vals, m)
    now = bufs[(STEPS - 1) % 2]
    for y in range(OWN, 2 * OWN):
        for j, (c, s) in enumerate(row_sums(now, y, m)):
            out[y - OWN, j] = (own[y - OWN, j] + c / coef[y, j]) + (s - 6.0 * c)


def adjoint(own, pair, other, coef, stay, total, ping, pong, finish):
    m = masks()
    for ref, row in strips(own, pair, other):
        for y in range(OWN):
            put(ping, row + y, [ref[y, j] for j in range(8)], m)
    bufs = (ping, pong)
    for k in range(1, STEPS + 1):
        now, later = bufs[(k - 1) % 2], bufs[k % 2]
        for y in range(k, EXT - k):
            vals = []
            for j, (c, s) in enumerate(row_sums(now, y, m)):
                w = stay[y, j] * c + coef[y, j] * s
                vals.append(w)
                if OWN <= y < 2 * OWN:
                    i = y - OWN
                    t = (own[i, j] if k == 1 else total[i, j]) + w
                    if k < STEPS:
                        total[i, j] = t
                    else:
                        finish(i, j, t)
            if k < STEPS:
                put(later, y, vals, m)


def back_row(y, j, probe):
    return pl.ds((j // 2) * 32 + probe * 16 + (j % 2) * 8 + y, 8, stride=128)


def adjoint_kernel(probe, own, pair, other, coef, stay, *refs):
    out, total, ping, pong = refs[-4:]

    def finish(y, j, t):
        out[back_row(y, j, probe)] = t

    adjoint(own, pair, other, coef, stay, total, ping, pong, finish)


def gram_kernel(back, probes, storage, flat, packed):
    for r in range(16):
        rows = pl.ds(r, 64, stride=16)
        y = (time_step * storage[r:r + 1, :]) * back[rows] + prior_weight * probes[rows]
        flat[:, r * 128:(r + 1) * 128] = y
    y = flat[...]
    gram = lax.dot_general(y, y, (((1,), (1,)), ((), ())), precision=lax.Precision.HIGHEST, preferred_element_type=f32)
    packed[...] = jnp.concatenate([gram[:32], gram[32:]], axis=1)


def solve_kernel(parts, flat, basis, factor, scale):
    dense = parts[0]
    for i in range(1, parts.shape[0]):
        dense = dense + parts[i]
    gram = jnp.concatenate([dense[:, :64], dense[:, 64:]], axis=0)
    row = lax.broadcasted_iota(jnp.int32, (64, 64), 0)
    col = lax.broadcasted_iota(jnp.int32, (64, 64), 1)
    eye = jnp.where(row == col, 1.0, 0.0)
    work = jnp.concatenate([gram, eye], axis=1)
    rows = lax.broadcasted_iota(jnp.int32, (64, 128), 0)
    diag = jnp.ones((64, 128), f32)
    for first in range(0, 64, 8):
        columns, factors, pivots = [], [], []
        for k in range(first, first + 8):
            column = jnp.broadcast_to(work[:, k:k + 1], (64, 128))
            pivot_row = work[k:k + 1, :]
            for c, f, p in zip(columns, factors, pivots):
                column = column - f * c[k:k + 1, :]
                pivot_row = pivot_row - f[k:k + 1, :] * p
            pivot = column[k:k + 1, :]
            diag = jnp.where(rows == k, pivot, diag)
            columns.append(column)
            factors.append(jnp.where(rows > k, column * (1.0 / pivot), 0.0))
            pivots.append(pivot_row)
        for f, p in zip(factors, pivots):
            work = work - f * p
    work = work * lax.rsqrt(diag)
    upper = jnp.where(row <= col, work[:, :64], 0.0)
    factor[...] = upper / scale
    inverse = work[:, 64:] * scale
    solved = lax.dot_general(inverse, flat[...], (((1,), (0,)), ((), ())), precision=lax.Precision.HIGHEST, preferred_element_type=f32)
    for r in range(16):
        basis[pl.ds(r, 64, stride=16)] = solved[:, r * 128:(r + 1) * 128]


def shape(*dims):
    return jax.ShapeDtypeStruct(dims, f32)


def call(kernel, outs, *args, scratch=(), sems=0, places=None, limit=32 * 1024 * 1024, flops=0, alias={}, name):
    spec = pl.BlockSpec(memory_space=pltpu.VMEM)
    many = isinstance(outs, tuple)
    return pl.pallas_call(
        kernel,
        out_shape=outs,
        in_specs=[pl.BlockSpec(memory_space=p) for p in places or [pltpu.VMEM] * len(args)],
        out_specs=tuple([spec] * len(outs)) if many else spec,
        scratch_shapes=[pltpu.VMEM(s, f32) for s in scratch] + [pltpu.SemaphoreType.DMA((sems,))] * (sems > 0),
        compiler_params=pltpu.CompilerParams(vmem_limit_bytes=limit),
        cost_estimate=pl.CostEstimate(flops=1024, bytes_accessed=1024, transcendentals=0),
        input_output_aliases=alias,
        name=name,
    )(*args)


def shards(probes, conduct, storage):
    probes, conduct, storage = probes.reshape(64, 16, 128), conduct.reshape(16, 128), storage.reshape(16, 128)
    sent = call(
        send_kernel,
        shape(32, CHUNK, 128),
        probes,
        conduct,
        storage,
        scratch=(probes.shape, conduct.shape, storage.shape),
        sems=3,
        places=[pltpu.HBM] * 3,
        limit=None,
        name="send",
    )
    got = lax.all_to_all(sent, ("ty", "tx", "tc"), 0, 0, tiled=True)
    field = shape(OWN, 8, 8, 128)
    got = got.reshape(32 * CHUNK, 128)
    half, first = call(pack_kernel, (shape(OWN, 4, 8, 128), field), got, name="pack")
    exchanges = [[(i, i + 1) for i in range(k, 7, 2)] for k in range(2)]
    exchanges = [e + [(j, i) for i, j in e] for e in exchanges]

    def sides(a):
        return [a] + [lax.ppermute(a, "tz", e) for e in exchanges]

    def swap(a):
        return lax.ppermute(a, "tc", [(0, 1), (1, 0)])

    halfs = sides(half)
    fields = [sides(first)]
    second = call(pack_second_kernel, field, got, fields[0][1], places=[pltpu.VMEM, pl.ANY], name="pack2")
    fields.append(sides(second))
    wide = shape(EXT, 8, 8, 128)
    coefs = call(coef_kernel, (wide, wide), *halfs, *[swap(a) for a in halfs], name="coef")
    pads = ((EXT, 10, 8, 128),) * 2
    work = 14 * 120 * 8 * 1024
    forward = [
        call(forward_kernel, field, *f, *coefs, scratch=(wide.shape,) + pads, flops=work, name="forward") for f in fields
    ]
    forward = [sides(f) for f in forward]
    scratch = (field.shape,) + pads
    summed = call(
        functools.partial(adjoint_kernel, 0), shape(1024, 128), *forward[0], *coefs, scratch=scratch, flops=work, name="adjoint1"
    )
    summed = call(
        functools.partial(adjoint_kernel, 1),
        shape(1024, 128),
        *forward[1],
        *coefs,
        summed,
        scratch=scratch,
        flops=work,
        alias={5: 0},
        name="adjoint2",
    )
    back = lax.all_to_all(summed.reshape(32, 32, 128), ("ty", "tx", "tc"), 0, 0, tiled=True)
    flat, gram = call(
        gram_kernel,
        (shape(64, 2048), shape(32, 128)),
        back.reshape(1024, 128),
        probes.reshape(1024, 128),
        storage,
        name="gram",
    )
    gram = gram + swap(gram)
    parts = lax.all_to_all(jnp.broadcast_to(gram[None], (16, 32, 128)), ("ty", "tx"), 0, 0, tiled=True)
    parts = lax.all_to_all(jnp.broadcast_to(parts.sum(0)[None], (8, 32, 128)), "tz", 0, 0, tiled=True)
    scale = math.sqrt(64 * 64 * 128)

    def solve(*refs):
        solve_kernel(*refs, scale)

    basis, factor = call(solve, (shape(1024, 128), shape(64, 64)), parts, flat, name="solve")
    return basis.reshape(64, 2, 8, 128), factor


def solution(mesh):
    fine = Mesh(mesh.devices.reshape(4, 4, 2, 8), ("ty", "tx", "tc", "tz"))
    gx = ("ty", "tx", "tc")
    placed = (P(None, gx, "tz", None), P(gx, "tz", None), P(gx, "tz", None))
    return jax.shard_map(
        shards,
        mesh=fine,
        in_specs=placed,
        out_specs=(P(None, gx, "tz", None), P()),
        check_vma=False,
    )
```

profile of v0, /device:TPU:2, one launch (start us, length us, event | category | flops | bytes accessed | tf_op | source)
XLA Modules:
  0.0 111.2 jit_solution(16588422774708718963)
XLA Ops:
  0.6 2.0 %send.1 = f32[32,40,128]{2,1,0:T(8,128)} custom-call(f32[64,16,128]{2,1,0:T(8,128)} %bitcast.11, f32[16,128]{1,0:T(8,128)} %bitcast.16, f32[16,128]{1,0:T(8,128)} %bitcast.14), custom_call_target="tpu_custom_call" | custom-call | flops 1024 | bytes 1024 | tf_op jit(solution)/shard_map/send/pallas_call | solution.py:210
  2.6 19.5 %all_to_all.20 = f32[32,40,128]{2,1,0:T(8,128)S(1)} all-to-all(f32[32,40,128]{2,1,0:T(8,128)} %send.1), channel_id=1, replica_groups=mesh['ty'=4,'tx'=4,'tc'=2,'tz'=8] {'ty','tx','tc'}, dimensions={0} | all-to-all | bytes 1310720 | tf_op jit(solution)/shard_map/all_to_all | solution.py:237
  22.1 0.2 pack.1
  22.4 2.0 %collective-permute-start = (f32[8,8,8,128]{3,2,1,0:T(8,128)S(1)}, f32[8,8,8,128]{3,2,1,0:T(8,128)S(1)}, u32[]{:S(2)}, u32[]{:S(2)}) collective-permute-start(f32[8,8,8,128]{3,2,1,0:T(8,128)S(1)} %get-tuple-element.10.own), channel_id=1, source_target_pairs={{0,1},{2,3},{4,5},{6,7},{1,0},{3,2},{5,4},{7,6},{8,9},{10,11},{12,... | collective-permute-start | bytes 786440 | tf_op jit(solution)/shard_map/ppermute | solution.py:245
  24.4 0.1 collective-permute-start.3
  24.5 0.7 collective-permute-start.4
  25.2 0.1 collective-permute-start.5
  25.3 0.7 collective-permute-start.10
  26.0 5.6 %collective-permute-done.arrived.pair = f32[8,8,8,128]{3,2,1,0:T(8,128)S(1)} collective-permute-done((f32[8,8,8,128]{3,2,1,0:T(8,128)S(1)}, f32[8,8,8,128]{3,2,1,0:T(8,128)S(1)}, u32[]{:S(2)}, u32[]{:S(2)}) %collective-permute-start) | collective-permute-done | bytes 262176 | tf_op jit(solution)/shard_map/ppermute | solution.py:245
  31.6 0.2 pack2.1.own
  31.7 2.0 %collective-permute-start.1 = (f32[8,8,8,128]{3,2,1,0:T(8,128)S(1)}, f32[8,8,8,128]{3,2,1,0:T(8,128)S(1)}, u32[]{:S(2)}, u32[]{:S(2)}) collective-permute-start(f32[8,8,8,128]{3,2,1,0:T(8,128)S(1)} %pack2.1.own), channel_id=1, source_target_pairs={{0,1},{2,3},{4,5},{6,7},{1,0},{3,2},{5,4},{7,6},{8,9},{10,11},{12,... | collective-permute-start | bytes 786440 | tf_op jit(solution)/shard_map/ppermute | solution.py:245
  33.8 0.3 collective-permute-done.3.m1
  34.0 0.7 collective-permute-start.2
  34.7 0.0 collective-permute-done.4.m2
  34.7 0.1 collective-permute-start.6
  34.8 0.0 collective-permute-done.5.t0
  34.8 0.5 collective-permute-start.7
  35.3 0.8 collective-permute-done.6.t1
  36.2 0.2 collective-permute-done.7.t2
  36.3 0.1 coef.1
  36.5 0.0 collective-permute-done.10.other
  36.5 2.2 %forward.3.own = f32[8,8,8,128]{3,2,1,0:T(8,128)S(1)} custom-call(f32[8,8,8,128]{3,2,1,0:T(8,128)S(1)} %get-tuple-element.10.own, f32[8,8,8,128]{3,2,1,0:T(8,128)S(1)} %collective-permute-done.arrived.pair, f32[8,8,8,128]{3,2,1,0:T(8,128)S(1)} %collective-permute-done.10.other, f32[24,8,8,128]{3,2,1,0:T(8,128)S(1)} %get-tuple-element.12.coef, ...), custom_call_target="tpu_custom_call" | custom-call | flops 1024 | bytes 1024 | tf_op jit(solution)/shard_map/forward/pallas_call | solution.py:210
  38.7 5.1 %collective-permute-start.11 = (f32[8,8,8,128]{3,2,1,0:T(8,128)S(1)}, f32[8,8,8,128]{3,2,1,0:T(8,128)S(1)}, u32[]{:S(2)}, u32[]{:S(2)}) collective-permute-start(f32[8,8,8,128]{3,2,1,0:T(8,128)S(1)} %forward.3.own), channel_id=1, source_target_pairs={{0,1},{2,3},{4,5},{6,7},{1,0},{3,2},{5,4},{7,6},{8,9},{10,11},{12,... | collective-permute-start | bytes 786440 | tf_op jit(solution)/shard_map/ppermute | solution.py:245
  43.8 0.7 collective-permute-start.12
  44.4 0.0 collective-permute-done.1.pair
  44.5 0.0 collective-permute-done.2.other
  44.5 2.2 %forward.2.own = f32[8,8,8,128]{3,2,1,0:T(8,128)S(1)} custom-call(f32[8,8,8,128]{3,2,1,0:T(8,128)S(1)} %pack2.1.own, f32[8,8,8,128]{3,2,1,0:T(8,128)S(1)} %collective-permute-done.1.pair, f32[8,8,8,128]{3,2,1,0:T(8,128)S(1)} %collective-permute-done.2.other, f32[24,8,8,128]{3,2,1,0:T(8,128)S(1)} %get-tuple-element.12.coef, ...), custom_call_target="tpu_custom_call" | custom-call | flops 1024 | bytes 1024 | tf_op jit(solution)/shard_map/forward/pallas_call | solution.py:210
  46.7 7.4 %collective-permute-start.8 = (f32[8,8,8,128]{3,2,1,0:T(8,128)S(1)}, f32[8,8,8,128]{3,2,1,0:T(8,128)S(1)}, u32[]{:S(2)}, u32[]{:S(2)}) collective-permute-start(f32[8,8,8,128]{3,2,1,0:T(8,128)S(1)} %forward.2.own), channel_id=1, source_target_pairs={{0,1},{2,3},{4,5},{6,7},{1,0},{3,2},{5,4},{7,6},{8,9},{10,11},{12,... | collective-permute-start | bytes 786440 | tf_op jit(solution)/shard_map/ppermute | solution.py:245
  54.1 0.8 collective-permute-start.9
  54.9 0.0 collective-permute-done.11.pair
  54.9 0.0 collective-permute-done.12.other
  54.9 2.1 %adjoint1.1.refs_0_ = f32[1024,128]{1,0:T(8,128)S(1)} custom-call(f32[8,8,8,128]{3,2,1,0:T(8,128)S(1)} %forward.3.own, f32[8,8,8,128]{3,2,1,0:T(8,128)S(1)} %collective-permute-done.11.pair, f32[8,8,8,128]{3,2,1,0:T(8,128)S(1)} %collective-permute-done.12.other, f32[24,8,8,128]{3,2,1,0:T(8,128)S(1)} %get-tuple-element.12.coef, ...), custom_call_target="tpu_custom_call" | custom-call | flops 1024 | bytes 1024 | tf_op jit(solution)/shard_map/adjoint1/pallas_call | solution.py:210
  57.1 2.2 %collective-permute-done.8.pair = f32[8,8,8,128]{3,2,1,0:T(8,128)S(1)} collective-permute-done((f32[8,8,8,128]{3,2,1,0:T(8,128)S(1)}, f32[8,8,8,128]{3,2,1,0:T(8,128)S(1)}, u32[]{:S(2)}, u32[]{:S(2)}) %collective-permute-start.8) | collective-permute-done | bytes 262176 | tf_op jit(solution)/shard_map/ppermute | solution.py:245
  59.3 0.0 collective-permute-done.9.other
  59.3 2.1 %adjoint2.1 = f32[1024,128]{1,0:T(8,128)S(1)} custom-call(f32[8,8,8,128]{3,2,1,0:T(8,128)S(1)} %forward.2.own, f32[8,8,8,128]{3,2,1,0:T(8,128)S(1)} %collective-permute-done.8.pair, f32[8,8,8,128]{3,2,1,0:T(8,128)S(1)} %collective-permute-done.9.other, f32[24,8,8,128]{3,2,1,0:T(8,128)S(1)} %get-tuple-element.12.coef, ...), custom_call_target="tpu_custom_call", output_to_operand_aliasing={{}: (5, {})} | custom-call | flops 1024 | bytes 1024 | tf_op jit(solution)/shard_map/adjoint2/pallas_call | solution.py:210
  61.4 0.0 copy-start
  61.4 0.0 copy-start.1
  61.4 15.2 %all_to_all.21 = f32[32,32,128]{2,1,0:T(8,128)S(1)} all-to-all(f32[32,32,128]{2,1,0:T(8,128)S(1)} %bitcast.10), channel_id=1, replica_groups=mesh['ty'=4,'tx'=4,'tc'=2,'tz'=8] {'ty','tx','tc'}, dimensions={0} | all-to-all | bytes 1048576 | tf_op jit(solution)/shard_map/all_to_all | solution.py:277
  76.6 0.0 copy-done
  76.6 0.0 copy-done.1
  76.6 0.8 gram.1
  77.4 0.4 collective-permute-start.13
  77.8 0.8 collective-permute-done.13
  78.7 12.3 %all_to_all.22 = f32[16,32,128]{2,1,0:T(8,128)S(1)} all-to-all(f32[16,32,128]{2,1,0:T(8,128)S(1)} %broadcast_in_dim.4), channel_id=1, replica_groups=mesh['ty'=4,'tx'=4,'tc'=2,'tz'=8] {'ty','tx'}, dimensions={0} | all-to-all | bytes 524288 | tf_op jit(solution)/shard_map/all_to_all | solution.py:287
  91.0 16.9 %all_to_all.23.refs_0_ = f32[8,32,128]{2,1,0:T(8,128)S(1)} all-to-all(f32[8,32,128]{2,1,0:T(8,128)S(1)} %broadcast_in_dim.5), channel_id=1, replica_groups=mesh['ty'=4,'tx'=4,'tc'=2,'tz'=8] {'tz'}, dimensions={0} | all-to-all | bytes 262144 | tf_op jit(solution)/shard_map/all_to_all | solution.py:288
  108.0 3.3 %solve.1 = (f32[1024,128]{1,0:T(8,128)}, f32[64,64]{1,0:T(8,128)}) custom-call(f32[8,32,128]{2,1,0:T(8,128)S(1)} %all_to_all.23.refs_0_, f32[64,2048]{1,0:T(8,128)S(1)} %get-tuple-element.15.refs_1_), custom_call_target="tpu_custom_call" | custom-call | flops 1024 | bytes 1024 | tf_op jit(solution)/shard_map/solve/pallas_call | solution.py:210
  (4 shorter events, 0.1 us)
Async XLA Ops:
  22.4 9.2 %collective-permute-start = (f32[8,8,8,128]{3,2,1,0:T(8,128)S(1)}, f32[8,8,8,128]{3,2,1,0:T(8,128)S(1)}, u32[]{:S(2)}, u32[]{:S(2)}) collective-permute-start(f32[8,8,8,128]{3,2,1,0:T(8,128)S(1)} %get-tuple-element.10.own), channel_id=1, source_target_pairs={{0,1},{2,3},{4,5},{6,7},{1,0},{3,2},{5,4},{7,6},{8,9},{10,11},{12,... | collective-permute-start | bytes 786440 | tf_op jit(solution)/shard_map/ppermute | solution.py:245
  24.4 9.7 %collective-permute-start.3 = (f32[8,4,8,128]{3,2,1,0:T(8,128)S(1)}, f32[8,4,8,128]{3,2,1,0:T(8,128)S(1)}, u32[]{:S(2)}, u32[]{:S(2)}) collective-permute-start(f32[8,4,8,128]{3,2,1,0:T(8,128)S(1)} %get-tuple-element.11.m0), channel_id=1, source_target_pairs={{0,1},{2,3},{4,5},{6,7},{1,0},{3,2},{5,4},{7,6},{8,9},{10,11},{12,... | collective-permute-start | bytes 393224 | tf_op jit(solution)/shard_map/ppermute | solution.py:245
  24.5 10.2 %collective-permute-start.4 = (f32[8,4,8,128]{3,2,1,0:T(8,128)S(1)}, f32[8,4,8,128]{3,2,1,0:T(8,128)S(1)}, u32[]{:S(2)}, u32[]{:S(2)}) collective-permute-start(f32[8,4,8,128]{3,2,1,0:T(8,128)S(1)} %get-tuple-element.11.m0), channel_id=1, source_target_pairs={{1,2},{3,4},{5,6},{2,1},{4,3},{6,5},{9,10},{11,12},{13,14},{10,9},... | collective-permute-start | bytes 393224 | tf_op jit(solution)/shard_map/ppermute | solution.py:245
  25.2 9.7 %collective-permute-start.5 = (f32[8,4,8,128]{3,2,1,0:T(8,128)S(1)}, f32[8,4,8,128]{3,2,1,0:T(8,128)S(1)}, u32[]{:S(2)}, u32[]{:S(2)}) collective-permute-start(f32[8,4,8,128]{3,2,1,0:T(8,128)S(1)} %get-tuple-element.11.m0), channel_id=1, source_target_pairs={{0,8},{8,0},{1,9},{9,1},{2,10},{10,2},{3,11},{11,3},{4,12},{12,4},... | collective-permute-start | bytes 393224 | tf_op jit(solution)/shard_map/ppermute | solution.py:248
  25.3 11.2 %collective-permute-start.10 = (f32[8,8,8,128]{3,2,1,0:T(8,128)S(1)}, f32[8,8,8,128]{3,2,1,0:T(8,128)S(1)}, u32[]{:S(2)}, u32[]{:S(2)}) collective-permute-start(f32[8,8,8,128]{3,2,1,0:T(8,128)S(1)} %get-tuple-element.10.own), channel_id=1, source_target_pairs={{1,2},{3,4},{5,6},{2,1},{4,3},{6,5},{9,10},{11,12},{13,14},{10,9},... | collective-permute-start | bytes 786440 | tf_op jit(solution)/shard_map/ppermute | solution.py:245
  31.7 12.7 %collective-permute-start.1 = (f32[8,8,8,128]{3,2,1,0:T(8,128)S(1)}, f32[8,8,8,128]{3,2,1,0:T(8,128)S(1)}, u32[]{:S(2)}, u32[]{:S(2)}) collective-permute-start(f32[8,8,8,128]{3,2,1,0:T(8,128)S(1)} %pack2.1.own), channel_id=1, source_target_pairs={{0,1},{2,3},{4,5},{6,7},{1,0},{3,2},{5,4},{7,6},{8,9},{10,11},{12,... | collective-permute-start | bytes 786440 | tf_op jit(solution)/shard_map/ppermute | solution.py:245
  34.0 10.4 %collective-permute-start.2 = (f32[8,8,8,128]{3,2,1,0:T(8,128)S(1)}, f32[8,8,8,128]{3,2,1,0:T(8,128)S(1)}, u32[]{:S(2)}, u32[]{:S(2)}) collective-permute-start(f32[8,8,8,128]{3,2,1,0:T(8,128)S(1)} %pack2.1.own), channel_id=1, source_target_pairs={{1,2},{3,4},{5,6},{2,1},{4,3},{6,5},{9,10},{11,12},{13,14},{10,9},... | collective-permute-start | bytes 786440 | tf_op jit(solution)/shard_map/ppermute | solution.py:245
  34.7 1.4 %collective-permute-start.6 = (f32[8,4,8,128]{3,2,1,0:T(8,128)S(1)}, f32[8,4,8,128]{3,2,1,0:T(8,128)S(1)}, u32[]{:S(2)}, u32[]{:S(2)}) collective-permute-start(f32[8,4,8,128]{3,2,1,0:T(8,128)S(1)} %collective-permute-done.3.m1), channel_id=1, source_target_pairs={{0,8},{8,0},{1,9},{9,1},{2,10},{10,2},{3,11},{11,3},{4,12},{12,4},... | collective-permute-start | bytes 393224 | tf_op jit(solution)/shard_map/ppermute | solution.py:248
  34.8 1.5 %collective-permute-start.7 = (f32[8,4,8,128]{3,2,1,0:T(8,128)S(1)}, f32[8,4,8,128]{3,2,1,0:T(8,128)S(1)}, u32[]{:S(2)}, u32[]{:S(2)}) collective-permute-start(f32[8,4,8,128]{3,2,1,0:T(8,128)S(1)} %collective-permute-done.4.m2), channel_id=1, source_target_pairs={{0,8},{8,0},{1,9},{9,1},{2,10},{10,2},{3,11},{11,3},{4,12},{12,4},... | collective-permute-start | bytes 393224 | tf_op jit(solution)/shard_map/ppermute | solution.py:248
  38.7 16.2 %collective-permute-start.11 = (f32[8,8,8,128]{3,2,1,0:T(8,128)S(1)}, f32[8,8,8,128]{3,2,1,0:T(8,128)S(1)}, u32[]{:S(2)}, u32[]{:S(2)}) collective-permute-start(f32[8,8,8,128]{3,2,1,0:T(8,128)S(1)} %forward.3.own), channel_id=1, source_target_pairs={{0,1},{2,3},{4,5},{6,7},{1,0},{3,2},{5,4},{7,6},{8,9},{10,11},{12,... | collective-permute-start | bytes 786440 | tf_op jit(solution)/shard_map/ppermute | solution.py:245
  43.8 11.1 %collective-permute-start.12 = (f32[8,8,8,128]{3,2,1,0:T(8,128)S(1)}, f32[8,8,8,128]{3,2,1,0:T(8,128)S(1)}, u32[]{:S(2)}, u32[]{:S(2)}) collective-permute-start(f32[8,8,8,128]{3,2,1,0:T(8,128)S(1)} %forward.3.own), channel_id=1, source_target_pairs={{1,2},{3,4},{5,6},{2,1},{4,3},{6,5},{9,10},{11,12},{13,14},{10,9},... | collective-permute-start | bytes 786440 | tf_op jit(solution)/shard_map/ppermute | solution.py:245
  46.7 12.6 %collective-permute-start.8 = (f32[8,8,8,128]{3,2,1,0:T(8,128)S(1)}, f32[8,8,8,128]{3,2,1,0:T(8,128)S(1)}, u32[]{:S(2)}, u32[]{:S(2)}) collective-permute-start(f32[8,8,8,128]{3,2,1,0:T(8,128)S(1)} %forward.2.own), channel_id=1, source_target_pairs={{0,1},{2,3},{4,5},{6,7},{1,0},{3,2},{5,4},{7,6},{8,9},{10,11},{12,... | collective-permute-start | bytes 786440 | tf_op jit(solution)/shard_map/ppermute | solution.py:245
  54.1 5.2 %collective-permute-start.9 = (f32[8,8,8,128]{3,2,1,0:T(8,128)S(1)}, f32[8,8,8,128]{3,2,1,0:T(8,128)S(1)}, u32[]{:S(2)}, u32[]{:S(2)}) collective-permute-start(f32[8,8,8,128]{3,2,1,0:T(8,128)S(1)} %forward.2.own), channel_id=1, source_target_pairs={{1,2},{3,4},{5,6},{2,1},{4,3},{6,5},{9,10},{11,12},{13,14},{10,9},... | collective-permute-start | bytes 786440 | tf_op jit(solution)/shard_map/ppermute | solution.py:245
  61.4 15.2 %copy-start = (f32[64,2,8,128]{3,2,1,0:T(8,128)S(1)}, f32[64,2,8,128]{3,2,1,0:T(8,128)}, u32[]{:S(2)}) copy-start(f32[64,2,8,128]{3,2,1,0:T(8,128)} %param.3) | copy-start | bytes 1572868
  61.4 15.2 %copy-start.1 = (f32[2,8,128]{2,1,0:T(8,128)S(1)}, f32[2,8,128]{2,1,0:T(8,128)}, u32[]{:S(2)}) copy-start(f32[2,8,128]{2,1,0:T(8,128)} %param.5) | copy-start | bytes 24580
  77.4 1.2 %collective-permute-start.13 = (f32[32,128]{1,0:T(8,128)S(1)}, f32[32,128]{1,0:T(8,128)S(1)}, u32[]{:S(2)}, u32[]{:S(2)}) collective-permute-start(f32[32,128]{1,0:T(8,128)S(1)} %get-tuple-element.14), channel_id=1, source_target_pairs={{0,8},{8,0},{1,9},{9,1},{2,10},{10,2},{3,11},{11,3},{4,12},{12,4},... | collective-permute-start | bytes 49160 | tf_op jit(solution)/shard_map/ppermute | solution.py:248
where the time goes:
time: 112 us; the launch traced here: 111 us
  blocking collectives  63.9 us (57%)
  starting transfers between devices  21.2 us (19%)
  Pallas kernels  15.2 us (14%)
  waiting for transfers between devices  9.97 us (9%)
    ppermute x10, starting transfers between devices, sides(): return [a] + [lax.ppermute(a, 'tz', e) for e in exchanges]  20.1 us
    all_to_all x1, blocking collectives, shards(): got = lax.all_to_all(sent, ('ty', 'tx', 'tc'), 0, 0, tiled=True)  19.5 us
    all_to_all x1, blocking collectives, shards(): lax.all_to_all(jnp.broadcast_to(parts.sum(0)[None], (8, 32, 128)), 'tz',...  16.9 us
    pallas_call x10, Pallas kernels, call(): pl.pallas_call(kernel, out_shape=outs, in_specs=[pl.BlockSpec(memory_spac...  15.2 us
    all_to_all x1, blocking collectives, shards(): lax.all_to_all(summed.reshape(32, 32, 128), ('ty', 'tx', 'tc'), 0, 0, til...  15.2 us
    all_to_all x1, blocking collectives, shards(): lax.all_to_all(jnp.broadcast_to(gram[None], (16, 32, 128)), ('ty', 'tx'),...  12.3 us
    ppermute x10, waiting for transfers between devices, sides(): return [a] + [lax.ppermute(a, 'tz', e) for e in exchanges]  8.11 us
  transfers between devices with their start and end apart: 14, of which 6 were waited for; matrix products, arithmetic and copies ran while one was open for 0% of the time, Pallas kernels for 6%

commit v1 on v0

--- a/solution.py
+++ b/solution.py
@@ -162,14 +162,28 @@
         flat[:, r * 128:(r + 1) * 128] = y
     y = flat[...]
     gram = lax.dot_general(y, y, (((1,), (1,)), ((), ())), precision=lax.Precision.HIGHEST, preferred_element_type=f32)
-    packed[...] = jnp.concatenate([gram[:32], gram[32:]], axis=1)
+    for i, block in enumerate((gram[:32, :32], gram[:32, 32:], gram[32:, 32:])):
+        packed[8 * i:8 * i + 8] = jnp.concatenate([block[8 * k:8 * k + 8] for k in range(4)], axis=1)
+
+
+def thirds(value):
+    parts = []
+    for _ in range(3):
+        parts.append(value.astype(jnp.bfloat16))
+        value = value - parts[-1].astype(f32)
+    return parts
 
 
 def solve_kernel(parts, flat, basis, factor, scale):
     dense = parts[0]
     for i in range(1, parts.shape[0]):
         dense = dense + parts[i]
-    gram = jnp.concatenate([dense[:, :64], dense[:, 64:]], axis=0)
+    blocks = [
+        jnp.concatenate([dense[8 * i:8 * i + 8, 32 * k:32 * k + 32] for k in range(4)], axis=0) for i in range(3)
+    ]
+    gram = jnp.concatenate(
+        [jnp.concatenate(blocks[:2], axis=1), jnp.concatenate([blocks[1].T, blocks[2]], axis=1)], axis=0
+    )
     row = lax.broadcasted_iota(jnp.int32, (64, 64), 0)
     col = lax.broadcasted_iota(jnp.int32, (64, 64), 1)
     eye = jnp.where(row == col, 1.0, 0.0)
@@ -195,7 +209,11 @@
     upper = jnp.where(row <= col, work[:, :64], 0.0)
     factor[...] = upper / scale
     inverse = work[:, 64:] * scale
-    solved = lax.dot_general(inverse, flat[...], (((1,), (0,)), ((), ())), precision=lax.Precision.HIGHEST, preferred_element_type=f32)
+    a, b = thirds(inverse), thirds(flat[...])
+    pairs = ((0, 0), (0, 1), (1, 0), (1, 1), (0, 2), (2, 0))
+    left = jnp.concatenate([a[i] for i, _ in pairs], axis=1)
+    right = jnp.concatenate([b[j] for _, j in pairs], axis=0)
+    solved = jnp.dot(left, right, preferred_element_type=f32)
     for r in range(16):
         basis[pl.ds(r, 64, stride=16)] = solved[:, r * 128:(r + 1) * 128]
 
@@ -277,15 +295,15 @@
     back = lax.all_to_all(summed.reshape(32, 32, 128), ("ty", "tx", "tc"), 0, 0, tiled=True)
     flat, gram = call(
         gram_kernel,
-        (shape(64, 2048), shape(32, 128)),
+        (shape(64, 2048), shape(24, 128)),
         back.reshape(1024, 128),
         probes.reshape(1024, 128),
         storage,
         name="gram",
     )
     gram = gram + swap(gram)
-    parts = lax.all_to_all(jnp.broadcast_to(gram[None], (16, 32, 128)), ("ty", "tx"), 0, 0, tiled=True)
-    parts = lax.all_to_all(jnp.broadcast_to(parts.sum(0)[None], (8, 32, 128)), "tz", 0, 0, tiled=True)
+    parts = lax.all_to_all(jnp.broadcast_to(gram[None], (16, 24, 128)), ("ty", "tx"), 0, 0, tiled=True)
+    parts = lax.all_to_all(jnp.broadcast_to(parts.sum(0)[None], (8, 24, 128)), "tz", 0, 0, tiled=True)
     scale = math.sqrt(64 * 64 * 128)
 
     def solve(*refs):

time: 112 us -> 111 us (level)
  no operation moved by 1% of the time
where the time goes in v1:
time: 111 us; the launch traced here: 110 us
  blocking collectives  62.9 us (57%)
  starting transfers between devices  21.3 us (19%)
  Pallas kernels  15.2 us (14%)
  waiting for transfers between devices  9.97 us (9%)
    ppermute x10, starting transfers between devices, sides(): return [a] + [lax.ppermute(a, 'tz', e) for e in exchanges]  20.1 us
    all_to_all x1, blocking collectives, shards(): got = lax.all_to_all(sent, ('ty', 'tx', 'tc'), 0, 0, tiled=True)  19.5 us
    all_to_all x1, blocking collectives, shards(): lax.all_to_all(jnp.broadcast_to(parts.sum(0)[None], (8, 24, 128)), 'tz',...  16.6 us
    pallas_call x10, Pallas kernels, call(): pl.pallas_call(kernel, out_shape=outs, in_specs=[pl.BlockSpec(memory_spac...  15.2 us
    all_to_all x1, blocking collectives, shards(): lax.all_to_all(summed.reshape(32, 32, 128), ('ty', 'tx', 'tc'), 0, 0, til...  15.2 us
    all_to_all x1, blocking collectives, shards(): lax.all_to_all(jnp.broadcast_to(gram[None], (16, 24, 128)), ('ty', 'tx'),...  11.6 us
    ppermute x10, waiting for transfers between devices, sides(): return [a] + [lax.ppermute(a, 'tz', e) for e in exchanges]  8.11 us
  transfers between devices with their start and end apart: 14, of which 6 were waited for; matrix products, arithmetic and copies ran while one was open for 0% of the time, Pallas kernels for 6%

profile of v1, /device:TPU:2, one launch (start us, length us, event | category | flops | bytes accessed | tf_op | source)
XLA Modules:
  0.0 110.2 jit_solution(17282499684560257745)
XLA Ops:
  0.6 2.0 %send.1 = f32[32,40,128]{2,1,0:T(8,128)} custom-call(f32[64,16,128]{2,1,0:T(8,128)} %bitcast.11, f32[16,128]{1,0:T(8,128)} %bitcast.16, f32[16,128]{1,0:T(8,128)} %bitcast.14), custom_call_target="tpu_custom_call" | custom-call | flops 1024 | bytes 1024 | tf_op jit(solution)/shard_map/send/pallas_call | solution.py:228
  2.6 19.5 %all_to_all.20 = f32[32,40,128]{2,1,0:T(8,128)S(1)} all-to-all(f32[32,40,128]{2,1,0:T(8,128)} %send.1), channel_id=1, replica_groups=mesh['ty'=4,'tx'=4,'tc'=2,'tz'=8] {'ty','tx','tc'}, dimensions={0} | all-to-all | bytes 1310720 | tf_op jit(solution)/shard_map/all_to_all | solution.py:255
  22.1 0.2 pack.1
  22.4 2.0 %collective-permute-start = (f32[8,8,8,128]{3,2,1,0:T(8,128)S(1)}, f32[8,8,8,128]{3,2,1,0:T(8,128)S(1)}, u32[]{:S(2)}, u32[]{:S(2)}) collective-permute-start(f32[8,8,8,128]{3,2,1,0:T(8,128)S(1)} %get-tuple-element.10.own), channel_id=1, source_target_pairs={{0,1},{2,3},{4,5},{6,7},{1,0},{3,2},{5,4},{7,6},{8,9},{10,11},{12,... | collective-permute-start | bytes 786440 | tf_op jit(solution)/shard_map/ppermute | solution.py:263
  24.4 0.1 collective-permute-start.3
  24.5 0.7 collective-permute-start.4
  25.2 0.1 collective-permute-start.5
  25.3 0.7 collective-permute-start.10
  26.0 5.6 %collective-permute-done.arrived.pair = f32[8,8,8,128]{3,2,1,0:T(8,128)S(1)} collective-permute-done((f32[8,8,8,128]{3,2,1,0:T(8,128)S(1)}, f32[8,8,8,128]{3,2,1,0:T(8,128)S(1)}, u32[]{:S(2)}, u32[]{:S(2)}) %collective-permute-start) | collective-permute-done | bytes 262176 | tf_op jit(solution)/shard_map/ppermute | solution.py:263
  31.6 0.2 pack2.1.own
  31.7 2.0 %collective-permute-start.1 = (f32[8,8,8,128]{3,2,1,0:T(8,128)S(1)}, f32[8,8,8,128]{3,2,1,0:T(8,128)S(1)}, u32[]{:S(2)}, u32[]{:S(2)}) collective-permute-start(f32[8,8,8,128]{3,2,1,0:T(8,128)S(1)} %pack2.1.own), channel_id=1, source_target_pairs={{0,1},{2,3},{4,5},{6,7},{1,0},{3,2},{5,4},{7,6},{8,9},{10,11},{12,... | collective-permute-start | bytes 786440 | tf_op jit(solution)/shard_map/ppermute | solution.py:263
  33.8 0.3 collective-permute-done.3.m1
  34.0 0.7 collective-permute-start.2
  34.7 0.0 collective-permute-done.4.m2
  34.7 0.1 collective-permute-start.6
  34.8 0.0 collective-permute-done.5.t0
  34.8 0.5 collective-permute-start.7
  35.3 0.8 collective-permute-done.6.t1
  36.2 0.2 collective-permute-done.7.t2
  36.3 0.1 coef.1
  36.5 0.0 collective-permute-done.10.other
  36.5 2.2 %forward.3.own = f32[8,8,8,128]{3,2,1,0:T(8,128)S(1)} custom-call(f32[8,8,8,128]{3,2,1,0:T(8,128)S(1)} %get-tuple-element.10.own, f32[8,8,8,128]{3,2,1,0:T(8,128)S(1)} %collective-permute-done.arrived.pair, f32[8,8,8,128]{3,2,1,0:T(8,128)S(1)} %collective-permute-done.10.other, f32[24,8,8,128]{3,2,1,0:T(8,128)S(1)} %get-tuple-element.12.coef, ...), custom_call_target="tpu_custom_call" | custom-call | flops 1024 | bytes 1024 | tf_op jit(solution)/shard_map/forward/pallas_call | solution.py:228
  38.7 5.1 %collective-permute-start.11 = (f32[8,8,8,128]{3,2,1,0:T(8,128)S(1)}, f32[8,8,8,128]{3,2,1,0:T(8,128)S(1)}, u32[]{:S(2)}, u32[]{:S(2)}) collective-permute-start(f32[8,8,8,128]{3,2,1,0:T(8,128)S(1)} %forward.3.own), channel_id=1, source_target_pairs={{0,1},{2,3},{4,5},{6,7},{1,0},{3,2},{5,4},{7,6},{8,9},{10,11},{12,... | collective-permute-start | bytes 786440 | tf_op jit(solution)/shard_map/ppermute | solution.py:263
  43.8 0.7 collective-permute-start.12
  44.4 0.0 collective-permute-done.1.pair
  44.5 0.0 collective-permute-done.2.other
  44.5 2.2 %forward.2.own = f32[8,8,8,128]{3,2,1,0:T(8,128)S(1)} custom-call(f32[8,8,8,128]{3,2,1,0:T(8,128)S(1)} %pack2.1.own, f32[8,8,8,128]{3,2,1,0:T(8,128)S(1)} %collective-permute-done.1.pair, f32[8,8,8,128]{3,2,1,0:T(8,128)S(1)} %collective-permute-done.2.other, f32[24,8,8,128]{3,2,1,0:T(8,128)S(1)} %get-tuple-element.12.coef, ...), custom_call_target="tpu_custom_call" | custom-call | flops 1024 | bytes 1024 | tf_op jit(solution)/shard_map/forward/pallas_call | solution.py:228
  46.7 7.4 %collective-permute-start.8 = (f32[8,8,8,128]{3,2,1,0:T(8,128)S(1)}, f32[8,8,8,128]{3,2,1,0:T(8,128)S(1)}, u32[]{:S(2)}, u32[]{:S(2)}) collective-permute-start(f32[8,8,8,128]{3,2,1,0:T(8,128)S(1)} %forward.2.own), channel_id=1, source_target_pairs={{0,1},{2,3},{4,5},{6,7},{1,0},{3,2},{5,4},{7,6},{8,9},{10,11},{12,... | collective-permute-start | bytes 786440 | tf_op jit(solution)/shard_map/ppermute | solution.py:263
  54.1 0.8 collective-permute-start.9
  54.9 0.0 collective-permute-done.11.pair
  54.9 0.0 collective-permute-done.12.other
  54.9 2.1 %adjoint1.1.refs_0_ = f32[1024,128]{1,0:T(8,128)S(1)} custom-call(f32[8,8,8,128]{3,2,1,0:T(8,128)S(1)} %forward.3.own, f32[8,8,8,128]{3,2,1,0:T(8,128)S(1)} %collective-permute-done.11.pair, f32[8,8,8,128]{3,2,1,0:T(8,128)S(1)} %collective-permute-done.12.other, f32[24,8,8,128]{3,2,1,0:T(8,128)S(1)} %get-tuple-element.12.coef, ...), custom_call_target="tpu_custom_call" | custom-call | flops 1024 | bytes 1024 | tf_op jit(solution)/shard_map/adjoint1/pallas_call | solution.py:228
  57.1 2.2 %collective-permute-done.8.pair = f32[8,8,8,128]{3,2,1,0:T(8,128)S(1)} collective-permute-done((f32[8,8,8,128]{3,2,1,0:T(8,128)S(1)}, f32[8,8,8,128]{3,2,1,0:T(8,128)S(1)}, u32[]{:S(2)}, u32[]{:S(2)}) %collective-permute-start.8) | collective-permute-done | bytes 262176 | tf_op jit(solution)/shard_map/ppermute | solution.py:263
  59.3 0.0 collective-permute-done.9.other
  59.3 2.1 %adjoint2.1 = f32[1024,128]{1,0:T(8,128)S(1)} custom-call(f32[8,8,8,128]{3,2,1,0:T(8,128)S(1)} %forward.2.own, f32[8,8,8,128]{3,2,1,0:T(8,128)S(1)} %collective-permute-done.8.pair, f32[8,8,8,128]{3,2,1,0:T(8,128)S(1)} %collective-permute-done.9.other, f32[24,8,8,128]{3,2,1,0:T(8,128)S(1)} %get-tuple-element.12.coef, ...), custom_call_target="tpu_custom_call", output_to_operand_aliasing={{}: (5, {})} | custom-call | flops 1024 | bytes 1024 | tf_op jit(solution)/shard_map/adjoint2/pallas_call | solution.py:228
  61.4 0.0 copy-start
  61.4 0.0 copy-start.1
  61.4 15.2 %all_to_all.21 = f32[32,32,128]{2,1,0:T(8,128)S(1)} all-to-all(f32[32,32,128]{2,1,0:T(8,128)S(1)} %bitcast.10), channel_id=1, replica_groups=mesh['ty'=4,'tx'=4,'tc'=2,'tz'=8] {'ty','tx','tc'}, dimensions={0} | all-to-all | bytes 1048576 | tf_op jit(solution)/shard_map/all_to_all | solution.py:295
  76.6 0.0 copy-done
  76.6 0.0 copy-done.1
  76.6 0.9 gram.1
  77.5 0.4 collective-permute-start.13
  78.0 0.8 collective-permute-done.13
  78.8 11.6 %all_to_all.22 = f32[16,24,128]{2,1,0:T(8,128)S(1)} all-to-all(f32[16,24,128]{2,1,0:T(8,128)S(1)} %broadcast_in_dim.4), channel_id=1, replica_groups=mesh['ty'=4,'tx'=4,'tc'=2,'tz'=8] {'ty','tx'}, dimensions={0} | all-to-all | bytes 393216 | tf_op jit(solution)/shard_map/all_to_all | solution.py:305
  90.4 16.6 %all_to_all.23.refs_0_ = f32[8,24,128]{2,1,0:T(8,128)S(1)} all-to-all(f32[8,24,128]{2,1,0:T(8,128)S(1)} %broadcast_in_dim.5), channel_id=1, replica_groups=mesh['ty'=4,'tx'=4,'tc'=2,'tz'=8] {'tz'}, dimensions={0} | all-to-all | bytes 196608 | tf_op jit(solution)/shard_map/all_to_all | solution.py:306
  107.0 3.2 %solve.1 = (f32[1024,128]{1,0:T(8,128)}, f32[64,64]{1,0:T(8,128)}) custom-call(f32[8,24,128]{2,1,0:T(8,128)S(1)} %all_to_all.23.refs_0_, f32[64,2048]{1,0:T(8,128)S(1)} %get-tuple-element.15.refs_1_), custom_call_target="tpu_custom_call" | custom-call | flops 1024 | bytes 1024 | tf_op jit(solution)/shard_map/solve/pallas_call | solution.py:228
  (4 shorter events, 0.1 us)
Async XLA Ops:
  22.4 9.2 %collective-permute-start = (f32[8,8,8,128]{3,2,1,0:T(8,128)S(1)}, f32[8,8,8,128]{3,2,1,0:T(8,128)S(1)}, u32[]{:S(2)}, u32[]{:S(2)}) collective-permute-start(f32[8,8,8,128]{3,2,1,0:T(8,128)S(1)} %get-tuple-element.10.own), channel_id=1, source_target_pairs={{0,1},{2,3},{4,5},{6,7},{1,0},{3,2},{5,4},{7,6},{8,9},{10,11},{12,... | collective-permute-start | bytes 786440 | tf_op jit(solution)/shard_map/ppermute | solution.py:263
  24.4 9.7 %collective-permute-start.3 = (f32[8,4,8,128]{3,2,1,0:T(8,128)S(1)}, f32[8,4,8,128]{3,2,1,0:T(8,128)S(1)}, u32[]{:S(2)}, u32[]{:S(2)}) collective-permute-start(f32[8,4,8,128]{3,2,1,0:T(8,128)S(1)} %get-tuple-element.11.m0), channel_id=1, source_target_pairs={{0,1},{2,3},{4,5},{6,7},{1,0},{3,2},{5,4},{7,6},{8,9},{10,11},{12,... | collective-permute-start | bytes 393224 | tf_op jit(solution)/shard_map/ppermute | solution.py:263
  24.5 10.2 %collective-permute-start.4 = (f32[8,4,8,128]{3,2,1,0:T(8,128)S(1)}, f32[8,4,8,128]{3,2,1,0:T(8,128)S(1)}, u32[]{:S(2)}, u32[]{:S(2)}) collective-permute-start(f32[8,4,8,128]{3,2,1,0:T(8,128)S(1)} %get-tuple-element.11.m0), channel_id=1, source_target_pairs={{1,2},{3,4},{5,6},{2,1},{4,3},{6,5},{9,10},{11,12},{13,14},{10,9},... | collective-permute-start | bytes 393224 | tf_op jit(solution)/shard_map/ppermute | solution.py:263
  25.2 9.7 %collective-permute-start.5 = (f32[8,4,8,128]{3,2,1,0:T(8,128)S(1)}, f32[8,4,8,128]{3,2,1,0:T(8,128)S(1)}, u32[]{:S(2)}, u32[]{:S(2)}) collective-permute-start(f32[8,4,8,128]{3,2,1,0:T(8,128)S(1)} %get-tuple-element.11.m0), channel_id=1, source_target_pairs={{0,8},{8,0},{1,9},{9,1},{2,10},{10,2},{3,11},{11,3},{4,12},{12,4},... | collective-permute-start | bytes 393224 | tf_op jit(solution)/shard_map/ppermute | solution.py:266
  25.3 11.2 %collective-permute-start.10 = (f32[8,8,8,128]{3,2,1,0:T(8,128)S(1)}, f32[8,8,8,128]{3,2,1,0:T(8,128)S(1)}, u32[]{:S(2)}, u32[]{:S(2)}) collective-permute-start(f32[8,8,8,128]{3,2,1,0:T(8,128)S(1)} %get-tuple-element.10.own), channel_id=1, source_target_pairs={{1,2},{3,4},{5,6},{2,1},{4,3},{6,5},{9,10},{11,12},{13,14},{10,9},... | collective-permute-start | bytes 786440 | tf_op jit(solution)/shard_map/ppermute | solution.py:263
  31.7 12.7 %collective-permute-start.1 = (f32[8,8,8,128]{3,2,1,0:T(8,128)S(1)}, f32[8,8,8,128]{3,2,1,0:T(8,128)S(1)}, u32[]{:S(2)}, u32[]{:S(2)}) collective-permute-start(f32[8,8,8,128]{3,2,1,0:T(8,128)S(1)} %pack2.1.own), channel_id=1, source_target_pairs={{0,1},{2,3},{4,5},{6,7},{1,0},{3,2},{5,4},{7,6},{8,9},{10,11},{12,... | collective-permute-start | bytes 786440 | tf_op jit(solution)/shard_map/ppermute | solution.py:263
  34.0 10.4 %collective-permute-start.2 = (f32[8,8,8,128]{3,2,1,0:T(8,128)S(1)}, f32[8,8,8,128]{3,2,1,0:T(8,128)S(1)}, u32[]{:S(2)}, u32[]{:S(2)}) collective-permute-start(f32[8,8,8,128]{3,2,1,0:T(8,128)S(1)} %pack2.1.own), channel_id=1, source_target_pairs={{1,2},{3,4},{5,6},{2,1},{4,3},{6,5},{9,10},{11,12},{13,14},{10,9},... | collective-permute-start | bytes 786440 | tf_op jit(solution)/shard_map/ppermute | solution.py:263
  34.7 1.4 %collective-permute-start.6 = (f32[8,4,8,128]{3,2,1,0:T(8,128)S(1)}, f32[8,4,8,128]{3,2,1,0:T(8,128)S(1)}, u32[]{:S(2)}, u32[]{:S(2)}) collective-permute-start(f32[8,4,8,128]{3,2,1,0:T(8,128)S(1)} %collective-permute-done.3.m1), channel_id=1, source_target_pairs={{0,8},{8,0},{1,9},{9,1},{2,10},{10,2},{3,11},{11,3},{4,12},{12,4},... | collective-permute-start | bytes 393224 | tf_op jit(solution)/shard_map/ppermute | solution.py:266
  34.8 1.5 %collective-permute-start.7 = (f32[8,4,8,128]{3,2,1,0:T(8,128)S(1)}, f32[8,4,8,128]{3,2,1,0:T(8,128)S(1)}, u32[]{:S(2)}, u32[]{:S(2)}) collective-permute-start(f32[8,4,8,128]{3,2,1,0:T(8,128)S(1)} %collective-permute-done.4.m2), channel_id=1, source_target_pairs={{0,8},{8,0},{1,9},{9,1},{2,10},{10,2},{3,11},{11,3},{4,12},{12,4},... | collective-permute-start | bytes 393224 | tf_op jit(solution)/shard_map/ppermute | solution.py:266
  38.7 16.2 %collective-permute-start.11 = (f32[8,8,8,128]{3,2,1,0:T(8,128)S(1)}, f32[8,8,8,128]{3,2,1,0:T(8,128)S(1)}, u32[]{:S(2)}, u32[]{:S(2)}) collective-permute-start(f32[8,8,8,128]{3,2,1,0:T(8,128)S(1)} %forward.3.own), channel_id=1, source_target_pairs={{0,1},{2,3},{4,5},{6,7},{1,0},{3,2},{5,4},{7,6},{8,9},{10,11},{12,... | collective-permute-start | bytes 786440 | tf_op jit(solution)/shard_map/ppermute | solution.py:263
  43.8 11.1 %collective-permute-start.12 = (f32[8,8,8,128]{3,2,1,0:T(8,128)S(1)}, f32[8,8,8,128]{3,2,1,0:T(8,128)S(1)}, u32[]{:S(2)}, u32[]{:S(2)}) collective-permute-start(f32[8,8,8,128]{3,2,1,0:T(8,128)S(1)} %forward.3.own), channel_id=1, source_target_pairs={{1,2},{3,4},{5,6},{2,1},{4,3},{6,5},{9,10},{11,12},{13,14},{10,9},... | collective-permute-start | bytes 786440 | tf_op jit(solution)/shard_map/ppermute | solution.py:263
  46.7 12.6 %collective-permute-start.8 = (f32[8,8,8,128]{3,2,1,0:T(8,128)S(1)}, f32[8,8,8,128]{3,2,1,0:T(8,128)S(1)}, u32[]{:S(2)}, u32[]{:S(2)}) collective-permute-start(f32[8,8,8,128]{3,2,1,0:T(8,128)S(1)} %forward.2.own), channel_id=1, source_target_pairs={{0,1},{2,3},{4,5},{6,7},{1,0},{3,2},{5,4},{7,6},{8,9},{10,11},{12,... | collective-permute-start | bytes 786440 | tf_op jit(solution)/shard_map/ppermute | solution.py:263
  54.1 5.2 %collective-permute-start.9 = (f32[8,8,8,128]{3,2,1,0:T(8,128)S(1)}, f32[8,8,8,128]{3,2,1,0:T(8,128)S(1)}, u32[]{:S(2)}, u32[]{:S(2)}) collective-permute-start(f32[8,8,8,128]{3,2,1,0:T(8,128)S(1)} %forward.2.own), channel_id=1, source_target_pairs={{1,2},{3,4},{5,6},{2,1},{4,3},{6,5},{9,10},{11,12},{13,14},{10,9},... | collective-permute-start | bytes 786440 | tf_op jit(solution)/shard_map/ppermute | solution.py:263
  61.4 15.2 %copy-start = (f32[64,2,8,128]{3,2,1,0:T(8,128)S(1)}, f32[64,2,8,128]{3,2,1,0:T(8,128)}, u32[]{:S(2)}) copy-start(f32[64,2,8,128]{3,2,1,0:T(8,128)} %param.3) | copy-start | bytes 1572868
  61.4 15.2 %copy-start.1 = (f32[2,8,128]{2,1,0:T(8,128)S(1)}, f32[2,8,128]{2,1,0:T(8,128)}, u32[]{:S(2)}) copy-start(f32[2,8,128]{2,1,0:T(8,128)} %param.5) | copy-start | bytes 24580
  77.5 1.2 %collective-permute-start.13 = (f32[24,128]{1,0:T(8,128)S(1)}, f32[24,128]{1,0:T(8,128)S(1)}, u32[]{:S(2)}, u32[]{:S(2)}) collective-permute-start(f32[24,128]{1,0:T(8,128)S(1)} %get-tuple-element.14), channel_id=1, source_target_pairs={{0,8},{8,0},{1,9},{9,1},{2,10},{10,2},{3,11},{11,3},{4,12},{12,4},... | collective-permute-start | bytes 36872 | tf_op jit(solution)/shard_map/ppermute | solution.py:266

commit v2 on v1

--- a/solution.py
+++ b/solution.py
@@ -161,7 +161,10 @@
         y = (time_step * storage[r:r + 1, :]) * back[rows] + prior_weight * probes[rows]
         flat[:, r * 128:(r + 1) * 128] = y
     y = flat[...]
-    gram = lax.dot_general(y, y, (((1,), (1,)), ((), ())), precision=lax.Precision.HIGHEST, preferred_element_type=f32)
+    stack = jnp.concatenate(thirds(y), axis=0)
+    p = lax.dot_general(stack, stack, (((1,), (1,)), ((), ())), preferred_element_type=f32)
+    low = (p[:64, 128:] + p[128:, :64]) + p[64:128, 64:128]
+    gram = p[:64, :64] + ((p[:64, 64:128] + p[64:128, :64]) + low)
     for i, block in enumerate((gram[:32, :32], gram[:32, 32:], gram[32:, 32:])):
         packed[8 * i:8 * i + 8] = jnp.concatenate([block[8 * k:8 * k + 8] for k in range(4)], axis=1)
 

time: 111 us -> 111 us (level)
  no operation moved by 1% of the time
where the time goes in v2:
time: 111 us; the launch traced here: 110 us
  blocking collectives  62.9 us (57%)
  starting transfers between devices  21.3 us (19%)
  Pallas kernels  15.2 us (14%)
  waiting for transfers between devices  9.97 us (9%)
    ppermute x10, starting transfers between devices, sides(): return [a] + [lax.ppermute(a, 'tz', e) for e in exchanges]  20.1 us
    all_to_all x1, blocking collectives, shards(): got = lax.all_to_all(sent, ('ty', 'tx', 'tc'), 0, 0, tiled=True)  19.5 us
    all_to_all x1, blocking collectives, shards(): lax.all_to_all(jnp.broadcast_to(parts.sum(0)[None], (8, 24, 128)), 'tz',...  16.6 us
    pallas_call x10, Pallas kernels, call(): pl.pallas_call(kernel, out_shape=outs, in_specs=[pl.BlockSpec(memory_spac...  15.2 us
    all_to_all x1, blocking collectives, shards(): lax.all_to_all(summed.reshape(32, 32, 128), ('ty', 'tx', 'tc'), 0, 0, til...  15.2 us
    all_to_all x1, blocking collectives, shards(): lax.all_to_all(jnp.broadcast_to(gram[None], (16, 24, 128)), ('ty', 'tx'),...  11.6 us
    ppermute x10, waiting for transfers between devices, sides(): return [a] + [lax.ppermute(a, 'tz', e) for e in exchanges]  8.11 us
  transfers between devices with their start and end apart: 14, of which 6 were waited for; matrix products, arithmetic and copies ran while one was open for 0% of the time, Pallas kernels for 6%

profile of v2, /device:TPU:2, one launch (start us, length us, event | category | flops | bytes accessed | tf_op | source)
XLA Modules:
  0.0 110.2 jit_solution(3869257310065977036)
XLA Ops:
  0.6 2.0 %send.1 = f32[32,40,128]{2,1,0:T(8,128)} custom-call(f32[64,16,128]{2,1,0:T(8,128)} %bitcast.11, f32[16,128]{1,0:T(8,128)} %bitcast.16, f32[16,128]{1,0:T(8,128)} %bitcast.14), custom_call_target="tpu_custom_call" | custom-call | flops 1024 | bytes 1024 | tf_op jit(solution)/shard_map/send/pallas_call | solution.py:231
  2.6 19.5 %all_to_all.20 = f32[32,40,128]{2,1,0:T(8,128)S(1)} all-to-all(f32[32,40,128]{2,1,0:T(8,128)} %send.1), channel_id=1, replica_groups=mesh['ty'=4,'tx'=4,'tc'=2,'tz'=8] {'ty','tx','tc'}, dimensions={0} | all-to-all | bytes 1310720 | tf_op jit(solution)/shard_map/all_to_all | solution.py:258
  22.1 0.2 pack.1
  22.4 2.0 %collective-permute-start = (f32[8,8,8,128]{3,2,1,0:T(8,128)S(1)}, f32[8,8,8,128]{3,2,1,0:T(8,128)S(1)}, u32[]{:S(2)}, u32[]{:S(2)}) collective-permute-start(f32[8,8,8,128]{3,2,1,0:T(8,128)S(1)} %get-tuple-element.10.own), channel_id=1, source_target_pairs={{0,1},{2,3},{4,5},{6,7},{1,0},{3,2},{5,4},{7,6},{8,9},{10,11},{12,... | collective-permute-start | bytes 786440 | tf_op jit(solution)/shard_map/ppermute | solution.py:266
  24.4 0.1 collective-permute-start.3
  24.5 0.7 collective-permute-start.4
  25.2 0.1 collective-permute-start.5
  25.3 0.7 collective-permute-start.10
  26.0 5.6 %collective-permute-done.arrived.pair = f32[8,8,8,128]{3,2,1,0:T(8,128)S(1)} collective-permute-done((f32[8,8,8,128]{3,2,1,0:T(8,128)S(1)}, f32[8,8,8,128]{3,2,1,0:T(8,128)S(1)}, u32[]{:S(2)}, u32[]{:S(2)}) %collective-permute-start) | collective-permute-done | bytes 262176 | tf_op jit(solution)/shard_map/ppermute | solution.py:266
  31.6 0.2 pack2.1.own
  31.7 2.0 %collective-permute-start.1 = (f32[8,8,8,128]{3,2,1,0:T(8,128)S(1)}, f32[8,8,8,128]{3,2,1,0:T(8,128)S(1)}, u32[]{:S(2)}, u32[]{:S(2)}) collective-permute-start(f32[8,8,8,128]{3,2,1,0:T(8,128)S(1)} %pack2.1.own), channel_id=1, source_target_pairs={{0,1},{2,3},{4,5},{6,7},{1,0},{3,2},{5,4},{7,6},{8,9},{10,11},{12,... | collective-permute-start | bytes 786440 | tf_op jit(solution)/shard_map/ppermute | solution.py:266
  33.8 0.3 collective-permute-done.3.m1
  34.0 0.7 collective-permute-start.2
  34.7 0.0 collective-permute-done.4.m2
  34.7 0.1 collective-permute-start.6
  34.8 0.0 collective-permute-done.5.t0
  34.8 0.5 collective-permute-start.7
  35.3 0.8 collective-permute-done.6.t1
  36.2 0.2 collective-permute-done.7.t2
  36.3 0.1 coef.1
  36.5 0.0 collective-permute-done.10.other
  36.5 2.2 %forward.3.own = f32[8,8,8,128]{3,2,1,0:T(8,128)S(1)} custom-call(f32[8,8,8,128]{3,2,1,0:T(8,128)S(1)} %get-tuple-element.10.own, f32[8,8,8,128]{3,2,1,0:T(8,128)S(1)} %collective-permute-done.arrived.pair, f32[8,8,8,128]{3,2,1,0:T(8,128)S(1)} %collective-permute-done.10.other, f32[24,8,8,128]{3,2,1,0:T(8,128)S(1)} %get-tuple-element.12.coef, ...), custom_call_target="tpu_custom_call" | custom-call | flops 1024 | bytes 1024 | tf_op jit(solution)/shard_map/forward/pallas_call | solution.py:231
  38.7 5.1 %collective-permute-start.11 = (f32[8,8,8,128]{3,2,1,0:T(8,128)S(1)}, f32[8,8,8,128]{3,2,1,0:T(8,128)S(1)}, u32[]{:S(2)}, u32[]{:S(2)}) collective-permute-start(f32[8,8,8,128]{3,2,1,0:T(8,128)S(1)} %forward.3.own), channel_id=1, source_target_pairs={{0,1},{2,3},{4,5},{6,7},{1,0},{3,2},{5,4},{7,6},{8,9},{10,11},{12,... | collective-permute-start | bytes 786440 | tf_op jit(solution)/shard_map/ppermute | solution.py:266
  43.8 0.7 collective-permute-start.12
  44.4 0.0 collective-permute-done.1.pair
  44.5 0.0 collective-permute-done.2.other
  44.5 2.2 %forward.2.own = f32[8,8,8,128]{3,2,1,0:T(8,128)S(1)} custom-call(f32[8,8,8,128]{3,2,1,0:T(8,128)S(1)} %pack2.1.own, f32[8,8,8,128]{3,2,1,0:T(8,128)S(1)} %collective-permute-done.1.pair, f32[8,8,8,128]{3,2,1,0:T(8,128)S(1)} %collective-permute-done.2.other, f32[24,8,8,128]{3,2,1,0:T(8,128)S(1)} %get-tuple-element.12.coef, ...), custom_call_target="tpu_custom_call" | custom-call | flops 1024 | bytes 1024 | tf_op jit(solution)/shard_map/forward/pallas_call | solution.py:231
  46.7 7.4 %collective-permute-start.8 = (f32[8,8,8,128]{3,2,1,0:T(8,128)S(1)}, f32[8,8,8,128]{3,2,1,0:T(8,128)S(1)}, u32[]{:S(2)}, u32[]{:S(2)}) collective-permute-start(f32[8,8,8,128]{3,2,1,0:T(8,128)S(1)} %forward.2.own), channel_id=1, source_target_pairs={{0,1},{2,3},{4,5},{6,7},{1,0},{3,2},{5,4},{7,6},{8,9},{10,11},{12,... | collective-permute-start | bytes 786440 | tf_op jit(solution)/shard_map/ppermute | solution.py:266
  54.1 0.8 collective-permute-start.9
  54.9 0.0 collective-permute-done.11.pair
  54.9 0.0 collective-permute-done.12.other
  54.9 2.1 %adjoint1.1.refs_0_ = f32[1024,128]{1,0:T(8,128)S(1)} custom-call(f32[8,8,8,128]{3,2,1,0:T(8,128)S(1)} %forward.3.own, f32[8,8,8,128]{3,2,1,0:T(8,128)S(1)} %collective-permute-done.11.pair, f32[8,8,8,128]{3,2,1,0:T(8,128)S(1)} %collective-permute-done.12.other, f32[24,8,8,128]{3,2,1,0:T(8,128)S(1)} %get-tuple-element.12.coef, ...), custom_call_target="tpu_custom_call" | custom-call | flops 1024 | bytes 1024 | tf_op jit(solution)/shard_map/adjoint1/pallas_call | solution.py:231
  57.1 2.2 %collective-permute-done.8.pair = f32[8,8,8,128]{3,2,1,0:T(8,128)S(1)} collective-permute-done((f32[8,8,8,128]{3,2,1,0:T(8,128)S(1)}, f32[8,8,8,128]{3,2,1,0:T(8,128)S(1)}, u32[]{:S(2)}, u32[]{:S(2)}) %collective-permute-start.8) | collective-permute-done | bytes 262176 | tf_op jit(solution)/shard_map/ppermute | solution.py:266
  59.3 0.0 collective-permute-done.9.other
  59.3 2.1 %adjoint2.1 = f32[1024,128]{1,0:T(8,128)S(1)} custom-call(f32[8,8,8,128]{3,2,1,0:T(8,128)S(1)} %forward.2.own, f32[8,8,8,128]{3,2,1,0:T(8,128)S(1)} %collective-permute-done.8.pair, f32[8,8,8,128]{3,2,1,0:T(8,128)S(1)} %collective-permute-done.9.other, f32[24,8,8,128]{3,2,1,0:T(8,128)S(1)} %get-tuple-element.12.coef, ...), custom_call_target="tpu_custom_call", output_to_operand_aliasing={{}: (5, {})} | custom-call | flops 1024 | bytes 1024 | tf_op jit(solution)/shard_map/adjoint2/pallas_call | solution.py:231
  61.4 0.0 copy-start
  61.4 0.0 copy-start.1
  61.4 15.2 %all_to_all.21 = f32[32,32,128]{2,1,0:T(8,128)S(1)} all-to-all(f32[32,32,128]{2,1,0:T(8,128)S(1)} %bitcast.10), channel_id=1, replica_groups=mesh['ty'=4,'tx'=4,'tc'=2,'tz'=8] {'ty','tx','tc'}, dimensions={0} | all-to-all | bytes 1048576 | tf_op jit(solution)/shard_map/all_to_all | solution.py:298
  76.6 0.0 copy-done
  76.6 0.0 copy-done.1
  76.6 0.9 gram.1
  77.5 0.4 collective-permute-start.13
  77.9 0.8 collective-permute-done.13
  78.8 11.6 %all_to_all.22 = f32[16,24,128]{2,1,0:T(8,128)S(1)} all-to-all(f32[16,24,128]{2,1,0:T(8,128)S(1)} %broadcast_in_dim.4), channel_id=1, replica_groups=mesh['ty'=4,'tx'=4,'tc'=2,'tz'=8] {'ty','tx'}, dimensions={0} | all-to-all | bytes 393216 | tf_op jit(solution)/shard_map/all_to_all | solution.py:308
  90.4 16.6 %all_to_all.23.refs_0_ = f32[8,24,128]{2,1,0:T(8,128)S(1)} all-to-all(f32[8,24,128]{2,1,0:T(8,128)S(1)} %broadcast_in_dim.5), channel_id=1, replica_groups=mesh['ty'=4,'tx'=4,'tc'=2,'tz'=8] {'tz'}, dimensions={0} | all-to-all | bytes 196608 | tf_op jit(solution)/shard_map/all_to_all | solution.py:309
  107.0 3.2 %solve.1 = (f32[1024,128]{1,0:T(8,128)}, f32[64,64]{1,0:T(8,128)}) custom-call(f32[8,24,128]{2,1,0:T(8,128)S(1)} %all_to_all.23.refs_0_, f32[64,2048]{1,0:T(8,128)S(1)} %get-tuple-element.15.refs_1_), custom_call_target="tpu_custom_call" | custom-call | flops 1024 | bytes 1024 | tf_op jit(solution)/shard_map/solve/pallas_call | solution.py:231
  (4 shorter events, 0.1 us)
Async XLA Ops:
  22.4 9.2 %collective-permute-start = (f32[8,8,8,128]{3,2,1,0:T(8,128)S(1)}, f32[8,8,8,128]{3,2,1,0:T(8,128)S(1)}, u32[]{:S(2)}, u32[]{:S(2)}) collective-permute-start(f32[8,8,8,128]{3,2,1,0:T(8,128)S(1)} %get-tuple-element.10.own), channel_id=1, source_target_pairs={{0,1},{2,3},{4,5},{6,7},{1,0},{3,2},{5,4},{7,6},{8,9},{10,11},{12,... | collective-permute-start | bytes 786440 | tf_op jit(solution)/shard_map/ppermute | solution.py:266
  24.4 9.7 %collective-permute-start.3 = (f32[8,4,8,128]{3,2,1,0:T(8,128)S(1)}, f32[8,4,8,128]{3,2,1,0:T(8,128)S(1)}, u32[]{:S(2)}, u32[]{:S(2)}) collective-permute-start(f32[8,4,8,128]{3,2,1,0:T(8,128)S(1)} %get-tuple-element.11.m0), channel_id=1, source_target_pairs={{0,1},{2,3},{4,5},{6,7},{1,0},{3,2},{5,4},{7,6},{8,9},{10,11},{12,... | collective-permute-start | bytes 393224 | tf_op jit(solution)/shard_map/ppermute | solution.py:266
  24.5 10.2 %collective-permute-start.4 = (f32[8,4,8,128]{3,2,1,0:T(8,128)S(1)}, f32[8,4,8,128]{3,2,1,0:T(8,128)S(1)}, u32[]{:S(2)}, u32[]{:S(2)}) collective-permute-start(f32[8,4,8,128]{3,2,1,0:T(8,128)S(1)} %get-tuple-element.11.m0), channel_id=1, source_target_pairs={{1,2},{3,4},{5,6},{2,1},{4,3},{6,5},{9,10},{11,12},{13,14},{10,9},... | collective-permute-start | bytes 393224 | tf_op jit(solution)/shard_map/ppermute | solution.py:266
  25.2 9.7 %collective-permute-start.5 = (f32[8,4,8,128]{3,2,1,0:T(8,128)S(1)}, f32[8,4,8,128]{3,2,1,0:T(8,128)S(1)}, u32[]{:S(2)}, u32[]{:S(2)}) collective-permute-start(f32[8,4,8,128]{3,2,1,0:T(8,128)S(1)} %get-tuple-element.11.m0), channel_id=1, source_target_pairs={{0,8},{8,0},{1,9},{9,1},{2,10},{10,2},{3,11},{11,3},{4,12},{12,4},... | collective-permute-start | bytes 393224 | tf_op jit(solution)/shard_map/ppermute | solution.py:269
  25.3 11.2 %collective-permute-start.10 = (f32[8,8,8,128]{3,2,1,0:T(8,128)S(1)}, f32[8,8,8,128]{3,2,1,0:T(8,128)S(1)}, u32[]{:S(2)}, u32[]{:S(2)}) collective-permute-start(f32[8,8,8,128]{3,2,1,0:T(8,128)S(1)} %get-tuple-element.10.own), channel_id=1, source_target_pairs={{1,2},{3,4},{5,6},{2,1},{4,3},{6,5},{9,10},{11,12},{13,14},{10,9},... | collective-permute-start | bytes 786440 | tf_op jit(solution)/shard_map/ppermute | solution.py:266
  31.7 12.7 %collective-permute-start.1 = (f32[8,8,8,128]{3,2,1,0:T(8,128)S(1)}, f32[8,8,8,128]{3,2,1,0:T(8,128)S(1)}, u32[]{:S(2)}, u32[]{:S(2)}) collective-permute-start(f32[8,8,8,128]{3,2,1,0:T(8,128)S(1)} %pack2.1.own), channel_id=1, source_target_pairs={{0,1},{2,3},{4,5},{6,7},{1,0},{3,2},{5,4},{7,6},{8,9},{10,11},{12,... | collective-permute-start | bytes 786440 | tf_op jit(solution)/shard_map/ppermute | solution.py:266
  34.0 10.4 %collective-permute-start.2 = (f32[8,8,8,128]{3,2,1,0:T(8,128)S(1)}, f32[8,8,8,128]{3,2,1,0:T(8,128)S(1)}, u32[]{:S(2)}, u32[]{:S(2)}) collective-permute-start(f32[8,8,8,128]{3,2,1,0:T(8,128)S(1)} %pack2.1.own), channel_id=1, source_target_pairs={{1,2},{3,4},{5,6},{2,1},{4,3},{6,5},{9,10},{11,12},{13,14},{10,9},... | collective-permute-start | bytes 786440 | tf_op jit(solution)/shard_map/ppermute | solution.py:266
  34.7 1.4 %collective-permute-start.6 = (f32[8,4,8,128]{3,2,1,0:T(8,128)S(1)}, f32[8,4,8,128]{3,2,1,0:T(8,128)S(1)}, u32[]{:S(2)}, u32[]{:S(2)}) collective-permute-start(f32[8,4,8,128]{3,2,1,0:T(8,128)S(1)} %collective-permute-done.3.m1), channel_id=1, source_target_pairs={{0,8},{8,0},{1,9},{9,1},{2,10},{10,2},{3,11},{11,3},{4,12},{12,4},... | collective-permute-start | bytes 393224 | tf_op jit(solution)/shard_map/ppermute | solution.py:269
  34.8 1.5 %collective-permute-start.7 = (f32[8,4,8,128]{3,2,1,0:T(8,128)S(1)}, f32[8,4,8,128]{3,2,1,0:T(8,128)S(1)}, u32[]{:S(2)}, u32[]{:S(2)}) collective-permute-start(f32[8,4,8,128]{3,2,1,0:T(8,128)S(1)} %collective-permute-done.4.m2), channel_id=1, source_target_pairs={{0,8},{8,0},{1,9},{9,1},{2,10},{10,2},{3,11},{11,3},{4,12},{12,4},... | collective-permute-start | bytes 393224 | tf_op jit(solution)/shard_map/ppermute | solution.py:269
  38.7 16.2 %collective-permute-start.11 = (f32[8,8,8,128]{3,2,1,0:T(8,128)S(1)}, f32[8,8,8,128]{3,2,1,0:T(8,128)S(1)}, u32[]{:S(2)}, u32[]{:S(2)}) collective-permute-start(f32[8,8,8,128]{3,2,1,0:T(8,128)S(1)} %forward.3.own), channel_id=1, source_target_pairs={{0,1},{2,3},{4,5},{6,7},{1,0},{3,2},{5,4},{7,6},{8,9},{10,11},{12,... | collective-permute-start | bytes 786440 | tf_op jit(solution)/shard_map/ppermute | solution.py:266
  43.8 11.1 %collective-permute-start.12 = (f32[8,8,8,128]{3,2,1,0:T(8,128)S(1)}, f32[8,8,8,128]{3,2,1,0:T(8,128)S(1)}, u32[]{:S(2)}, u32[]{:S(2)}) collective-permute-start(f32[8,8,8,128]{3,2,1,0:T(8,128)S(1)} %forward.3.own), channel_id=1, source_target_pairs={{1,2},{3,4},{5,6},{2,1},{4,3},{6,5},{9,10},{11,12},{13,14},{10,9},... | collective-permute-start | bytes 786440 | tf_op jit(solution)/shard_map/ppermute | solution.py:266
  46.7 12.6 %collective-permute-start.8 = (f32[8,8,8,128]{3,2,1,0:T(8,128)S(1)}, f32[8,8,8,128]{3,2,1,0:T(8,128)S(1)}, u32[]{:S(2)}, u32[]{:S(2)}) collective-permute-start(f32[8,8,8,128]{3,2,1,0:T(8,128)S(1)} %forward.2.own), channel_id=1, source_target_pairs={{0,1},{2,3},{4,5},{6,7},{1,0},{3,2},{5,4},{7,6},{8,9},{10,11},{12,... | collective-permute-start | bytes 786440 | tf_op jit(solution)/shard_map/ppermute | solution.py:266
  54.1 5.2 %collective-permute-start.9 = (f32[8,8,8,128]{3,2,1,0:T(8,128)S(1)}, f32[8,8,8,128]{3,2,1,0:T(8,128)S(1)}, u32[]{:S(2)}, u32[]{:S(2)}) collective-permute-start(f32[8,8,8,128]{3,2,1,0:T(8,128)S(1)} %forward.2.own), channel_id=1, source_target_pairs={{1,2},{3,4},{5,6},{2,1},{4,3},{6,5},{9,10},{11,12},{13,14},{10,9},... | collective-permute-start | bytes 786440 | tf_op jit(solution)/shard_map/ppermute | solution.py:266
  61.4 15.2 %copy-start = (f32[64,2,8,128]{3,2,1,0:T(8,128)S(1)}, f32[64,2,8,128]{3,2,1,0:T(8,128)}, u32[]{:S(2)}) copy-start(f32[64,2,8,128]{3,2,1,0:T(8,128)} %param.3) | copy-start | bytes 1572868
  61.4 15.2 %copy-start.1 = (f32[2,8,128]{2,1,0:T(8,128)S(1)}, f32[2,8,128]{2,1,0:T(8,128)}, u32[]{:S(2)}) copy-start(f32[2,8,128]{2,1,0:T(8,128)} %param.5) | copy-start | bytes 24580
  77.5 1.2 %collective-permute-start.13 = (f32[24,128]{1,0:T(8,128)S(1)}, f32[24,128]{1,0:T(8,128)S(1)}, u32[]{:S(2)}, u32[]{:S(2)}) collective-permute-start(f32[24,128]{1,0:T(8,128)S(1)} %get-tuple-element.14), channel_id=1, source_target_pairs={{0,8},{8,0},{1,9},{9,1},{2,10},{10,2},{3,11},{11,3},{4,12},{12,4},... | collective-permute-start | bytes 36872 | tf_op jit(solution)/shard_map/ppermute | solution.py:269
